TPU v7x, 32 devices: a whole 2x2x4 slice. The times are simulated.
32 devices in a mesh: ctx: 8 (over z, core), fsdp: 4 (over y, x).
Axes of the slice: x: 2, y: 2, z: 4, core: 2. Of those that a mesh axis runs over, the one named last changes fastest.
Arguments:
- inputs: bfloat16 [4, 4096, 1280], P('fsdp', 'ctx'), may hold values from -6 to 6
- cotangent: bfloat16 [4, 4096, 1280], P('fsdp', 'ctx'), may hold values from -6 to 6
- block_order: int32 [4, 16], P('fsdp'), may hold values from 0 to 15, each once within a row
- w_qkv: float32 [1280, 3840], P('fsdp'), may hold values from -0.15625 to 0.15625
- m_qkv: float32 [1280, 3840], P('fsdp'), may hold values from -768 to 768
- v_qkv: float32 [1280, 3840], P('fsdp'), may hold values from 16384 to 65536
- w_out: float32 [1280, 1280], P('fsdp'), may hold values from -2.5 to 2.5
- m_out: float32 [1280, 1280], P('fsdp'), may hold values from -64 to 64
- v_out: float32 [1280, 1280], P('fsdp'), may hold values from 124 to 496
- w_up: float32 [1280, 1280], P('fsdp'), may hold values from -0.15625 to 0.15625
- m_up: float32 [1280, 1280], P('fsdp'), may hold values from -384 to 384
- v_up: float32 [1280, 1280], P('fsdp'), may hold values from 4096 to 16384
- w_down: float32 [1280, 1280], P('fsdp'), may hold values from -0.15625 to 0.15625
- m_down: float32 [1280, 1280], P('fsdp'), may hold values from -448 to 448
- v_down: float32 [1280, 1280], P('fsdp'), may hold values from 5898.24 to 23592.96
- small_params: float32 [2640], replicated, may hold values from -1 to 2, as said below
- small_m: float32 [2640], replicated, may hold values from -576 to 576
- small_v: float32 [2640], replicated, may hold values from 4096 to 147456
Outputs:
- output: bfloat16 [4, 4096, 1280], P('fsdp', 'ctx')
- input_grad: bfloat16 [4, 4096, 1280], P('fsdp', 'ctx')
- qkv_new: float32 [1280, 3840], P('fsdp')
- qkv_first: float32 [1280, 3840], P('fsdp')
- qkv_second: float32 [1280, 3840], P('fsdp')
- qkv_low: bfloat16 [1280, 3840], P('fsdp')
- out_new: float32 [1280, 1280], P('fsdp')
- out_first: float32 [1280, 1280], P('fsdp')
- out_second: float32 [1280, 1280], P('fsdp')
- out_low: bfloat16 [1280, 1280], P('fsdp')
- up_new: float32 [1280, 1280], P('fsdp')
- up_first: float32 [1280, 1280], P('fsdp')
- up_second: float32 [1280, 1280], P('fsdp')
- up_low: bfloat16 [1280, 1280], P('fsdp')
- down_new: float32 [1280, 1280], P('fsdp')
- down_first: float32 [1280, 1280], P('fsdp')
- down_second: float32 [1280, 1280], P('fsdp')
- down_low: bfloat16 [1280, 1280], P('fsdp')
- small_new: float32 [2640], replicated
- small_first: float32 [2640], replicated
- small_second: float32 [2640], replicated
Inputs may be any that keep to these rules, and one draw needn't show every extreme that they name: `block_order`: each row lists the 16 causal blocks of its group once each. ctx index c holds the blocks at entries 2 c to 2 c + 1, in that order. Blocks below 8 form the prompt in order; block 8 + j is part (j % 2) of continuation j // 2. `small_params`: entries 0 to 2559 are gains; the last 80 are query scale parameters.
All inputs are finite; a program needn't handle non-finite values.
Results may differ from a plain program's by a relative error of at most 0.025.
Values may be sent and summed in bfloat16 or wider, within the bound.
A program may use at most 384 MiB of HBM per device.

v0:
```python
import functools
import math
import jax
import jax.numpy as jnp
from jax import lax
from jax.sharding import PartitionSpec as P

D = 1280
H = 16
HD = 80
FF = 1280
BLOCK = 256
CONT = 512
STEP = 3
norm_eps = 1e-06
beta_one = 0.5
beta_two = 0.5
adam_eps = 1e-08
decay_rate = 0.1
small_rate = 0.75
qkv_rate_base = 1.0
scale_base = 1.442695


def token_layout(block_ids):
    num_blocks = block_ids.shape[0]
    prompt_blocks = num_blocks // 2
    cont_blocks = CONT // BLOCK
    later = block_ids - prompt_blocks
    block_seg = jnp.where(block_ids < prompt_blocks, 0, 1 + later // cont_blocks)
    block_base = jnp.where(
        block_ids < prompt_blocks, block_ids * BLOCK, (prompt_blocks + later % cont_blocks) * BLOCK
    )
    offset = jnp.arange(BLOCK, dtype=jnp.int32)
    seg_ids = jnp.broadcast_to(block_seg[:, None], (num_blocks, BLOCK)).reshape(-1)
    positions = (block_base[:, None] + offset[None, :]).reshape(-1)
    return (seg_ids, positions)


def pair_mask(seg_query, pos_query, seg_key, pos_key):
    same_doc = (seg_key[None, :] == 0) | (seg_key[None, :] == seg_query[:, None])
    return (same_doc & (pos_key[None, :] <= pos_query[:, None]))[None]


def rms_scale(values):
    return lax.rsqrt(jnp.mean(values * values, axis=-1, keepdims=True) + norm_eps)


def head_scores(query_heads, key_heads):
    return jnp.einsum("qhd,khd->hqk", query_heads, key_heads, preferred_element_type=jnp.float32)


def adamw(weight, first, second, gradient, step_rate, decay_on):
    first_new = beta_one * first + (1.0 - beta_one) * gradient
    second_new = beta_two * second + (1.0 - beta_two) * gradient * gradient
    corr_one = 1.0 - beta_one**STEP
    corr_two = 1.0 - beta_two**STEP
    update = first_new / corr_one / (jnp.sqrt(second_new / corr_two) + adam_eps)
    weight_new = weight - step_rate * (update + decay_on * weight)
    return (weight_new, first_new, second_new)


def body(
    inputs,
    cotangent,
    block_order,
    w_qkv,
    m_qkv,
    v_qkv,
    w_out,
    m_out,
    v_out,
    w_up,
    m_up,
    v_up,
    w_down,
    m_down,
    v_down,
    small_params,
    small_m,
    small_v,
):
    rows_dev = inputs.shape[1]
    bf16 = jnp.bfloat16
    f32 = jnp.float32
    qkv_full, out_full, up_full, down_full = (
        lax.all_gather(w_qkv.astype(bf16), "fsdp", axis=0, tiled=True),
        lax.all_gather(w_out.astype(bf16), "fsdp", axis=0, tiled=True),
        lax.all_gather(w_up.astype(bf16), "fsdp", axis=0, tiled=True),
        lax.all_gather(w_down.astype(bf16), "fsdp", axis=0, tiled=True),
    )
    seg_all, pos_all = token_layout(block_order[0])
    here_row = lax.axis_index("ctx") * rows_dev
    seg_here = lax.dynamic_slice_in_dim(seg_all, here_row, rows_dev, 0)
    pos_here = lax.dynamic_slice_in_dim(pos_all, here_row, rows_dev, 0)
    gain_one = small_params[:D]
    gain_two = small_params[D : 2 * D]
    query_scale = small_params[2 * D :]
    layer_in = inputs[0].astype(f32)
    scale_one = rms_scale(layer_in)
    unit_one = layer_in * scale_one
    normed = (unit_one * gain_one).astype(bf16)
    qkv = jnp.dot(normed, qkv_full, preferred_element_type=f32)
    factor = scale_base / math.sqrt(HD) * jax.nn.softplus(query_scale)
    query_raw = qkv[:, :D].reshape(rows_dev, H, HD)
    queries = (query_raw * factor).astype(bf16)
    keys_here = qkv[:, D : 2 * D].astype(bf16)
    values_here = qkv[:, 2 * D :].astype(bf16)
    keys_all, values_all = (
        lax.all_gather(keys_here, "ctx", axis=0, tiled=True),
        lax.all_gather(values_here, "ctx", axis=0, tiled=True),
    )
    key_total = keys_all.shape[0]
    key_block = math.gcd(key_total, 512)
    num_blocks = key_total // key_block
    key_stack = (
        keys_all.reshape(num_blocks, key_block, H, HD),
        values_all.reshape(num_blocks, key_block, H, HD),
        seg_all.reshape(num_blocks, key_block),
        pos_all.reshape(num_blocks, key_block),
    )

    def stat_step(running, key_set):
        row_top, row_mass = running
        scores = head_scores(queries, key_set[0])
        allowed = pair_mask(seg_here, pos_here, key_set[2], key_set[3])
        block_top = jnp.max(jnp.where(allowed, scores, -1e30), axis=-1)
        new_top = jnp.maximum(row_top, block_top)
        row_mass = row_mass * jnp.exp(row_top - new_top) + jnp.sum(
            jnp.where(allowed, jnp.exp(scores - new_top[..., None]), 0.0), axis=-1
        )
        return ((new_top, row_mass), None)

    start_stats = (jnp.full((H, rows_dev), -1e30, f32), jnp.zeros((H, rows_dev), f32))
    (row_top, row_mass), unused = lax.scan(stat_step, start_stats, key_stack)
    row_lse = row_top + jnp.log(row_mass)

    def value_step(mixed_acc, key_set):
        scores = head_scores(queries, key_set[0])
        allowed = pair_mask(seg_here, pos_here, key_set[2], key_set[3])
        prob_rows = jnp.where(allowed, jnp.exp(scores - row_lse[..., None]), 0.0).astype(bf16)
        return (
            mixed_acc
            + jnp.einsum("hqk,khd->qhd", prob_rows, key_set[1], preferred_element_type=f32),
            None,
        )

    mixed, unused = lax.scan(value_step, jnp.zeros((rows_dev, H, HD), f32), key_stack)
    attn_low = mixed.reshape(rows_dev, D).astype(bf16)
    mid = layer_in + jnp.dot(attn_low, out_full, preferred_element_type=f32)
    scale_two = rms_scale(mid)
    unit_two = mid * scale_two
    normed_two = (unit_two * gain_two).astype(bf16)
    hidden = jnp.dot(normed_two, up_full, preferred_element_type=f32)
    gate_sig = jax.nn.sigmoid(hidden)
    act = (hidden * gate_sig).astype(bf16)
    output = (mid + jnp.dot(act, down_full, preferred_element_type=f32)).astype(bf16)
    grad_in = cotangent[0]
    grad_down = jnp.dot(act.T, grad_in, preferred_element_type=f32)
    dact = jnp.dot(grad_in, down_full.T, preferred_element_type=f32)
    dhidden = (dact * gate_sig * (1.0 + hidden * (1.0 - gate_sig))).astype(bf16)
    grad_up = jnp.dot(normed_two.T, dhidden, preferred_element_type=f32)
    dnormed_two = jnp.dot(dhidden, up_full.T, preferred_element_type=f32)
    dunit_two = dnormed_two * gain_two
    dmid = grad_in.astype(f32) + scale_two * (
        dunit_two - unit_two * jnp.mean(dunit_two * unit_two, axis=-1, keepdims=True)
    )
    gain_two_grad = jnp.sum(dnormed_two * unit_two, axis=0)
    dbranch = dmid.astype(bf16)
    grad_out = jnp.dot(attn_low.T, dbranch, preferred_element_type=f32)
    dattn = jnp.dot(dbranch, out_full.T, preferred_element_type=f32).astype(bf16)
    dattn_heads = dattn.reshape(rows_dev, H, HD)
    row_delta = jnp.sum(dattn_heads.astype(f32) * mixed, axis=-1).T

    def back_step(dq_acc, key_set, want_keys):
        scores = head_scores(queries, key_set[0])
        allowed = pair_mask(seg_here, pos_here, key_set[2], key_set[3])
        prob_rows = jnp.where(allowed, jnp.exp(scores - row_lse[..., None]), 0.0)
        grad_probs = jnp.einsum("qhd,khd->hqk", dattn_heads, key_set[1], preferred_element_type=f32)
        grad_scores = (prob_rows * (grad_probs - row_delta[..., None])).astype(bf16)
        dq_acc = dq_acc + jnp.einsum(
            "hqk,khd->qhd", grad_scores, key_set[0], preferred_element_type=f32
        )
        grad_keys = jnp.einsum("hqk,qhd->khd", grad_scores, queries, preferred_element_type=f32)
        grad_values = jnp.einsum(
            "hqk,qhd->khd", prob_rows.astype(bf16), dattn_heads, preferred_element_type=f32
        )
        return (dq_acc, (grad_keys.reshape(-1, D), grad_values.reshape(-1, D)))

    dq_start = jnp.zeros((rows_dev, H, HD), f32)
    dq_acc, key_parts = lax.scan(functools.partial(back_step, want_keys=True), dq_start, key_stack)
    dkeys_all = key_parts[0].reshape(key_total, D)
    dvalues_all = key_parts[1].reshape(key_total, D)
    dkeys_here, dvalues_here = (
        lax.psum_scatter(
            dkeys_all.astype(jnp.bfloat16), "ctx", scatter_dimension=0, tiled=True
        ).astype(jnp.float32),
        lax.psum_scatter(
            dvalues_all.astype(jnp.bfloat16), "ctx", scatter_dimension=0, tiled=True
        ).astype(jnp.float32),
    )
    dqkv = jnp.concatenate(
        [(dq_acc * factor).reshape(rows_dev, D), dkeys_here, dvalues_here], axis=1
    ).astype(bf16)
    scale_grad = (
        jnp.sum(dq_acc * query_raw, axis=(0, 1))
        * (scale_base / math.sqrt(HD))
        * jax.nn.sigmoid(query_scale)
    )
    grad_qkv = jnp.dot(normed.T, dqkv, preferred_element_type=f32)
    dnormed = jnp.dot(dqkv, qkv_full.T, preferred_element_type=f32)
    dunit_one = dnormed * gain_one
    input_grad = dmid + scale_one * (
        dunit_one - unit_one * jnp.mean(dunit_one * unit_one, axis=-1, keepdims=True)
    )
    gain_one_grad = jnp.sum(dnormed * unit_one, axis=0)
    small_grad = jnp.concatenate([gain_one_grad, gain_two_grad, scale_grad])
    small_total = lax.psum(small_grad, ("ctx", "fsdp"))
    rate_qkv = qkv_rate_base / math.sqrt(D)
    rate_out = 0.5 / math.sqrt(max(D // 256, 1))
    rate_up = 0.5 / math.sqrt(D)
    rate_down = 0.5 / math.sqrt(FF)
    shard_qkv, shard_out, shard_up, shard_down = (
        lax.psum_scatter(
            grad_qkv.astype(jnp.bfloat16), "fsdp", scatter_dimension=0, tiled=True
        ).astype(jnp.float32),
        lax.psum_scatter(
            grad_out.astype(jnp.bfloat16), "fsdp", scatter_dimension=0, tiled=True
        ).astype(jnp.float32),
        lax.psum_scatter(
            grad_up.astype(jnp.bfloat16), "fsdp", scatter_dimension=0, tiled=True
        ).astype(jnp.float32),
        lax.psum_scatter(
            grad_down.astype(jnp.bfloat16), "fsdp", scatter_dimension=0, tiled=True
        ).astype(jnp.float32),
    )
    total_qkv, total_out, total_up, total_down = (
        lax.psum(shard_qkv.astype(jnp.bfloat16), "ctx").astype(jnp.float32),
        lax.psum(shard_out.astype(jnp.bfloat16), "ctx").astype(jnp.float32),
        lax.psum(shard_up.astype(jnp.bfloat16), "ctx").astype(jnp.float32),
        lax.psum(shard_down.astype(jnp.bfloat16), "ctx").astype(jnp.float32),
    )
    qkv_set = adamw(w_qkv, m_qkv, v_qkv, total_qkv, rate_qkv, decay_rate)
    out_set = adamw(w_out, m_out, v_out, total_out, rate_out, decay_rate)
    up_set = adamw(w_up, m_up, v_up, total_up, rate_up, decay_rate)
    down_set = adamw(w_down, m_down, v_down, total_down, rate_down, decay_rate)
    small_set = adamw(small_params, small_m, small_v, small_total, small_rate, 0.0)
    return (
        output[None],
        input_grad.astype(bf16)[None],
        qkv_set[0],
        qkv_set[1],
        qkv_set[2],
        qkv_set[0].astype(bf16),
        out_set[0],
        out_set[1],
        out_set[2],
        out_set[0].astype(bf16),
        up_set[0],
        up_set[1],
        up_set[2],
        up_set[0].astype(bf16),
        down_set[0],
        down_set[1],
        down_set[2],
        down_set[0].astype(bf16),
        small_set[0],
        small_set[1],
        small_set[2],
    )


def solution(mesh):
    in_specs = (
        P("fsdp", "ctx", None),
        P("fsdp", "ctx", None),
        P("fsdp", None),
        P("fsdp", None),
        P("fsdp", None),
        P("fsdp", None),
        P("fsdp", None),
        P("fsdp", None),
        P("fsdp", None),
        P("fsdp", None),
        P("fsdp", None),
        P("fsdp", None),
        P("fsdp", None),
        P("fsdp", None),
        P("fsdp", None),
        P(),
        P(),
        P(),
    )
    out_specs = (
        P("fsdp", "ctx", None),
        P("fsdp", "ctx", None),
        P("fsdp", None),
        P("fsdp", None),
        P("fsdp", None),
        P("fsdp", None),
        P("fsdp", None),
        P("fsdp", None),
        P("fsdp", None),
        P("fsdp", None),
        P("fsdp", None),
        P("fsdp", None),
        P("fsdp", None),
        P("fsdp", None),
        P("fsdp", None),
        P("fsdp", None),
        P("fsdp", None),
        P("fsdp", None),
        P(),
        P(),
        P(),
    )
    return jax.shard_map(body, mesh=mesh, in_specs=in_specs, out_specs=out_specs, check_vma=False)
```

profile of v0, /device:TPU:0, one launch (start us, length us, event | category | flops | bytes accessed | tf_op | source)
XLA Modules:
  0.0 1684.8 jit_solution(14041899212990422532)
XLA Ops:
  13.6 100.2 %all-gather.7.cloned.1.call-done = bf16[1280,3840]{1,0:T(8,128)(2,1)} async-done(((bf16[320,3840]{1,0:T(8,128)(2,1)}), bf16[1280,3840]{1,0:T(8,128)(2,1)}) %all-gather.7.cloned.1.call-update) | async-done | bytes 9830416 | tf_op jit(solution)/shard_map/all_gather | solution.py:87
  113.8 11.3 fusion.97
  143.0 83.4 %all-gather.11.cloned.1.call-done = bf16[4096,1280]{1,0:T(8,128)(2,1)} async-done(((bf16[512,1280]{1,0:T(8,128)(2,1)}), bf16[4096,1280]{1,0:T(8,128)(2,1)}) %all-gather.11.cloned.1.call-update) | async-done | bytes 10485776 | tf_op jit(solution)/shard_map/all_gather | solution.py:110
  226.4 14.5 copy.59
  240.9 15.1 copy.93
  256.0 16.3 copy.63
  272.3 11.7 copy.61
  284.0 42.4 %all-gather.9.cloned.1.call-done = bf16[4096,1280]{1,0:T(8,128)(2,1)} async-done(((bf16[512,1280]{1,0:T(8,128)(2,1)}), bf16[4096,1280]{1,0:T(8,128)(2,1)}) %all-gather.9.cloned.1.call-update) | async-done | bytes 10485776 | tf_op jit(solution)/shard_map/all_gather | solution.py:111
  326.4 29.8 %reshape.410 = bf16[8,512,16,80]{3,2,1,0:T(8,128)(2,1)} reshape(bf16[4096,1280]{1,0:T(8,128)(2,1)} %all-gather.9.cloned.1.call-done) | data formatting | bytes 20971520 | tf_op jit(solution)/shard_map/reshape | solution.py:118
  356.2 21.7 %copy.62 = bf16[8,512,16,80]{1,3,2,0:T(8,128)(2,1)} copy(bf16[8,512,16,80]{3,2,1,0:T(8,128)(2,1)} %reshape.410) | data formatting | bytes 20971520
  378.0 150.4 %while.39 = (s32[]{:T(128)}, f32[16,512]{1,0:T(8,128)S(1)}, f32[16,512]{1,0:T(8,128)S(1)}, s32[8,512]{1,0:T(8,128)S(1)}, s32[512]{0:T(512)S(1)}, /*index=5*/s32[...) while((s32[]{:T(128)}, f32[16,512]{1,0:T(8,128)S(1)}, ...), condition=%wide.region_4.5_spmd.clone, body=%wide.region_1.4_spmd.clone.sunk | while | flops 693150208 | bytes 37405832 | solution.py:135
  378.3 9.6 fusion.140
  397.0 9.5 fusion.140
  415.7 9.5 fusion.140
  425.2 9.4 fusion.141
  435.1 9.5 fusion.140
  444.7 9.2 fusion.141
  454.3 9.5 fusion.140
  472.9 9.5 fusion.140
  491.5 9.5 fusion.140
  510.1 9.5 fusion.140
  528.4 95.0 %while.40 = (s32[]{:T(128)}, f32[512,16,80]{0,2,1:T(8,128)}, bf16[8,512,16,80]{1,3,2,0:T(8,128)(2,1)}, s32[8,512]{1,0:T(8,128)S(1)}, s32[512]{0:T(512)S(1)}, /*i...) while((s32[]{:T(128)}, f32[512,16,80]{0,2,1:T(8,128)}, ...), condition=%wide.region_6.7_spmd.clone, body=%wide.region_5.6_spmd.clone.sunk | while | flops 1357120000 | bytes 13157527 | solution.py:148
  543.1 8.8 bitcast_add_fusion.4
  555.0 8.8 bitcast_add_fusion.4
  566.9 8.8 bitcast_add_fusion.4
  578.8 8.8 bitcast_add_fusion.4
  590.7 8.8 bitcast_add_fusion.4
  602.6 8.8 bitcast_add_fusion.4
  655.5 418.3 %while.41 = (s32[]{:T(128)}, f32[512,16,80]{0,2,1:T(8,128)}, bf16[8,512,1280]{2,1,0:T(8,128)(2,1)}, bf16[8,512,1280]{2,1,0:T(8,128)(2,1)}, bf16[8,512,16,80]{1,3...) while((s32[]{:T(128)}, f32[512,16,80]{0,2,1:T(8,128)}, ...), condition=%wide.region_11.12_spmd.clone, body=%wide.region_10.11_spmd.clone.sunk | while | flops 3391357440 | bytes 103924920 | solution.py:191
  655.5 9.5 fusion.156
  665.3 11.1 fusion.157
  683.1 9.9 fusion.158
  707.2 9.5 fusion.156
  717.0 11.1 fusion.157
  735.5 9.9 fusion.158
  759.5 9.5 fusion.156
  769.4 11.1 fusion.157
  787.9 9.9 fusion.158
  811.9 9.5 fusion.156
  821.8 11.1 fusion.157
  840.3 9.9 fusion.158
  864.3 9.5 fusion.156
  874.1 11.1 fusion.157
  892.6 9.9 fusion.158
  916.6 9.5 fusion.156
  926.4 11.1 fusion.157
  944.9 9.9 fusion.158
  968.9 9.5 fusion.156
  978.8 11.1 fusion.157
  997.3 9.9 fusion.158
  1021.3 9.5 fusion.156
  1031.1 11.1 fusion.157
  1049.6 9.9 fusion.158
  1100.8 81.0 %reduce-scatter.9.cloned.1.call-done = bf16[512,1280]{1,0:T(8,128)(2,1)} async-done(((bf16[4096,1280]{1,0:T(8,128)(2,1)}), bf16[512,1280]{1,0:T(8,128)(2,1)}) %reduce-scatter.9.cloned.1.call-update) | async-done | bytes 1310736 | tf_op jit(solution)/shard_map/reduce_scatter | solution.py:198
  1181.9 110.1 %reduce-scatter.7.cloned.1.call-done = bf16[512,1280]{1,0:T(8,128)(2,1)} async-done(((bf16[4096,1280]{1,0:T(8,128)(2,1)}), bf16[512,1280]{1,0:T(8,128)(2,1)}) %reduce-scatter.7.cloned.1.call-update) | async-done | bytes 1310736 | tf_op jit(solution)/shard_map/reduce_scatter | solution.py:195
  1292.0 9.7 convolution_convert_fusion
  1309.2 29.8 %reduce-scatter.13.cloned.1.call-done = bf16[320,1280]{1,0:T(8,128)(2,1)} async-done(((bf16[1280,1280]{1,0:T(8,128)(2,1)}), bf16[320,1280]{1,0:T(8,128)(2,1)}) %reduce-scatter.13.cloned.1.call-update) | async-done | bytes 819216 | tf_op jit(solution)/shard_map/reduce_scatter | solution.py:227
  1339.0 48.5 %reduce-scatter.15.cloned.1.call-done = bf16[320,1280]{1,0:T(8,128)(2,1)} async-done(((bf16[1280,1280]{1,0:T(8,128)(2,1)}), bf16[320,1280]{1,0:T(8,128)(2,1)}) %reduce-scatter.15.cloned.1.call-update) | async-done | bytes 819216 | tf_op jit(solution)/shard_map/reduce_scatter | solution.py:230
  1387.6 48.7 %reduce-scatter.17.cloned.1.call-done = bf16[320,1280]{1,0:T(8,128)(2,1)} async-done(((bf16[1280,1280]{1,0:T(8,128)(2,1)}), bf16[320,1280]{1,0:T(8,128)(2,1)}) %reduce-scatter.17.cloned.1.call-update) | async-done | bytes 819216 | tf_op jit(solution)/shard_map/reduce_scatter | solution.py:233
  1436.3 101.2 %reduce-scatter.11.cloned.1.call-done = bf16[320,3840]{1,0:T(8,128)(2,1)} async-done(((bf16[1280,3840]{1,0:T(8,128)(2,1)}), bf16[320,3840]{1,0:T(8,128)(2,1)}) %reduce-scatter.11.cloned.1.call-update) | async-done | bytes 2457616 | tf_op jit(solution)/shard_map/reduce_scatter | solution.py:224
  1537.6 10.9 fusion.56
  1548.5 41.0 %psum.39 = f32[2640]{0:T(1024)S(1)} all-reduce(f32[2640]{0:T(1024)S(1)} %pad_maximum_fusion.3), channel_id=1, replica_groups=mesh['ctx'=8,'fsdp'=4] {'ctx','fsdp'}, use_global_device_ids=true, to_apply=%region_26.27 | all-reduce | flops 2640 | bytes 21120 | tf_op jit(solution)/shard_map/psum | solution.py:218
  1594.4 57.9 %all-reduce.3.cloned.1.call-done = (bf16[320,3840]{1,0:T(8,128)(2,1)}, bf16[320,1280]{1,0:T(8,128)(2,1)}, bf16[320,1280]{1,0:T(8,128)(2,1)}, bf16[320,1280]{1,0:T(8,128)(2,1)}) async-done(((bf16[320,3840]{1,0:T(8,128)(2,1)}, bf16[320,1280]{1,0:T(8,128)(2,1)}, bf16[320,1280]{1,0:T(8,128)(2,1)}, bf16[320,1280]{1,0:T(8,128)(2,1)}), (bf16[320,3840]{1,0:T(8,128)(2,1)}, bf16[320,1280]{1,0:T(8,128)(2,1)}, ...) | async-done | bytes 4915216 | tf_op jit(solution)/shard_map/psum | solution.py:238
  1652.4 12.6 fusion.93
  (333 shorter events, 379.8 us)
Async XLA Ops:
  7.2 106.6 %all-gather.7.cloned.1.call-start = ((), (), s32[]{:S(2)}) async-start(), calls=%async_computation.6 | async-start | bytes 12288000 | tf_op jit(solution)/shard_map/all_gather | solution.py:87
  11.3 1.3 copy-start.1
  11.3 1.7 copy-start.26
  11.3 215.0 %all-gather.11.cloned.1.call-start = ((), (), s32[]{:S(2)}) async-start(), calls=%async_computation.8 | async-start | bytes 11796480 | tf_op jit(solution)/shard_map/all_gather | solution.py:110
  13.0 112.2 %copy-start.37 = (f32[512]{0:T(512)}, f32[512]{0:T(512)S(1)}, u32[]{:S(2)}) copy-start(f32[512]{0:T(512)S(1)} %add_rsqrt_fusion.1) | copy-start | bytes 6148
  13.6 111.5 %copy-start.30 = (f32[1280]{0:T(1024)}, f32[1280]{0:T(1024)S(1)}, u32[]{:S(2)}) copy-start(f32[1280]{0:T(1024)S(1)} %get-tuple-element.485) | copy-start | bytes 15364
  126.8 1.4 copy-start.9
  126.8 2.5 copy-start.11
  126.8 199.6 %all-gather.9.cloned.1.call-start = ((), (), s32[]{:S(2)}) async-start(), calls=%async_computation.7 | async-start | bytes 11796480 | tf_op jit(solution)/shard_map/all_gather | solution.py:111
  127.6 498.9 %all-gather.13.cloned.1.call-start = ((), (), s32[]{:S(2)}) async-start(), calls=%async_computation.9 | async-start | bytes 4096000 | tf_op jit(solution)/shard_map/all_gather | solution.py:88
  129.2 1.7 copy-start.13
  129.2 503.1 %all-gather.15.cloned.1.call-start = ((), (), s32[]{:S(2)}) async-start(), calls=%async_computation.10 | async-start | bytes 4096000 | tf_op jit(solution)/shard_map/all_gather | solution.py:89
  130.3 2.2 copy-start.42
  130.3 508.4 %all-gather.17.cloned.1.call-start = ((), (), s32[]{:S(2)}) async-start(), calls=%async_computation.11 | async-start | bytes 4096000 | tf_op jit(solution)/shard_map/all_gather | solution.py:90
  131.9 1050.0 %reduce-scatter.9.cloned.1.call-start = ((), (), s32[]{:S(2)}) async-start(), calls=%async_computation.13 | async-start | bytes 11796480 | tf_op jit(solution)/shard_map/reduce_scatter | solution.py:198
  132.6 5.3 copy-start.39
  623.3 3.1 copy-start.2
  626.4 5.9 copy-start.28
  632.3 14.2 copy-start.34
  632.3 6.3 copy-start.21
  638.7 5.1 copy-start.5
  638.7 5.1 copy-start.41
  643.8 2.6 copy-start.43
  646.5 2.7 copy-start.4
  647.1 1.5 copy-start.7
  1073.8 218.3 %reduce-scatter.7.cloned.1.call-start = ((), (), s32[]{:S(2)}) async-start(), calls=%async_computation.12 | async-start | bytes 11796480 | tf_op jit(solution)/shard_map/reduce_scatter | solution.py:195
  1073.8 1.7 copy-start.8
  1074.5 264.5 %reduce-scatter.13.cloned.1.call-start = ((), (), s32[]{:S(2)}) async-start(), calls=%async_computation.15 | async-start | bytes 4096000 | tf_op jit(solution)/shard_map/reduce_scatter | solution.py:227
  1080.4 1.7 copy-start.6
  1080.4 1.7 copy-start.29
  1080.4 1.7 copy-start.35
  1080.5 307.1 %reduce-scatter.15.cloned.1.call-start = ((), (), s32[]{:S(2)}) async-start(), calls=%async_computation.16 | async-start | bytes 4096000 | tf_op jit(solution)/shard_map/reduce_scatter | solution.py:230
  1087.2 1.3 copy-start.22
  1087.2 349.0 %reduce-scatter.17.cloned.1.call-start = ((), (), s32[]{:S(2)}) async-start(), calls=%async_computation.17 | async-start | bytes 4096000 | tf_op jit(solution)/shard_map/reduce_scatter | solution.py:233
  1093.9 1.8 copy-start
  1093.9 1.8 copy-start.40
  1094.0 443.5 %reduce-scatter.11.cloned.1.call-start = ((), (), s32[]{:S(2)}) async-start(), calls=%async_computation.14 | async-start | bytes 12288000 | tf_op jit(solution)/shard_map/reduce_scatter | solution.py:224
  1099.1 192.9 %copy-start.3 = (bf16[1,512,1280]{2,1,0:T(8,128)(2,1)S(1)}, bf16[1,512,1280]{2,1,0:T(8,128)(2,1)}, u32[]{:S(2)}) copy-start(bf16[1,512,1280]{2,1,0:T(8,128)(2,1)} %param.24) | copy-start | bytes 3932164
  1099.1 192.9 %copy-start.31 = (f32[1280]{0:T(1024)S(1)}, f32[1280]{0:T(1024)}, u32[]{:S(2)}) copy-start(f32[1280]{0:T(1024)} %copy-done.30) | copy-start | bytes 15364
  1099.1 192.9 %copy-start.38 = (f32[512]{0:T(512)S(1)}, f32[512]{0:T(512)}, u32[]{:S(2)}) copy-start(f32[512]{0:T(512)} %copy-done.37) | copy-start | bytes 6148
  1301.7 0.7 copy-start.27
  1301.8 350.6 %all-reduce.3.cloned.1.call-start = ((), (), s32[]{:S(2)}) async-start(), calls=%async_computation.18 | async-start | bytes 9830400 | tf_op jit(solution)/shard_map/psum | solution.py:238
  1537.5 10.9 copy-start.36
  1537.5 51.9 %copy-start.32 = (f32[2640]{0:T(1024)S(1)}, f32[2640]{0:T(1024)}, u32[]{:S(2)}) copy-start(f32[2640]{0:T(1024)} %param.40) | copy-start | bytes 31684
  1537.6 51.9 %copy-start.33 = (f32[2640]{0:T(1024)S(1)}, f32[2640]{0:T(1024)}, u32[]{:S(2)}) copy-start(f32[2640]{0:T(1024)} %param.41) | copy-start | bytes 31684
  1652.4 12.6 copy-start.10
  1652.4 12.6 copy-start.15
  1652.4 12.6 copy-start.16
  1652.4 13.0 copy-start.25
  1665.4 3.4 copy-start.12
  1665.4 3.4 copy-start.17
  1665.4 4.5 copy-start.18
  1665.4 4.7 copy-start.24
  1670.0 3.4 copy-start.14
  1670.0 3.4 copy-start.19
  1670.0 4.5 copy-start.20
  1670.0 4.7 copy-start.23
Sparse Core Ops, SparseCore 0:
  11.5 102.2 all-gather.6
  126.9 99.3 all-gather.10
  228.6 97.7 all-gather.8
  328.7 43.4 all-gather.12
  374.4 45.0 all-gather.14
  421.8 45.0 all-gather.16
  1073.9 107.9 reduce-scatter.8
  1184.2 107.7 reduce-scatter.6
  1295.6 43.3 reduce-scatter.12
  1342.5 45.0 reduce-scatter.14
  1391.2 45.0 reduce-scatter.16
  1439.2 98.2 reduce-scatter.10
  1540.1 112.2 all-reduce.2
where the time goes:
time: 1690 us; the launch traced here: 1680 us
  waiting for transfers between devices  705 us (42%)
  matrix products  582 us (34%)
  local copies, waits for them, and re-layouts  208 us (12%)
  other arithmetic  132 us (8%)
  blocking collectives  41 us (2%)
    dot_general x16, matrix products, head_scores(): jnp.einsum('qhd,khd->hqk', query_heads, key_heads, preferred_element_type...  152 us
    reduce_scatter x1, waiting for transfers between devices, body(): lax.psum_scatter(dkeys_all.astype(jnp.bfloat16), 'ctx', scatter_dimension...  110 us
    reduce_scatter x1, waiting for transfers between devices, body(): lax.psum_scatter(grad_qkv.astype(jnp.bfloat16), 'fsdp', scatter_dimension...  101 us
    all_gather x1, waiting for transfers between devices, body(): lax.all_gather(w_qkv.astype(bf16), 'fsdp', axis=0, tiled=True)  100 us
    dot_general x8, matrix products, back_step(): jnp.einsum('qhd,khd->hqk', dattn_heads, key_set[1], preferred_element_typ...  88.4 us
    all_gather x1, waiting for transfers between devices, body(): lax.all_gather(keys_here, 'ctx', axis=0, tiled=True)  83.4 us
    reduce_scatter x1, waiting for transfers between devices, body(): lax.psum_scatter(dvalues_all.astype(jnp.bfloat16), 'ctx', scatter_dimensi...  81 us
    unnamed x97, local copies, waits for them, and re-layouts  81 us
  transfers between devices with their start and end apart: 13, of which 10 were waited for; matrix products, arithmetic and copies ran while one was open for 26% of the time, Pallas kernels for 0%

commit v1 on v0

--- a/solution.py
+++ b/solution.py
@@ -235,7 +235,7 @@
         ).astype(jnp.float32),
     )
     total_qkv, total_out, total_up, total_down = (
-        lax.psum(shard_qkv.astype(jnp.bfloat16), "ctx").astype(jnp.float32),
+        jnp.sum(lax.all_gather(shard_qkv.astype(jnp.bfloat16), "ctx"), axis=0).astype(jnp.float32),
         lax.psum(shard_out.astype(jnp.bfloat16), "ctx").astype(jnp.float32),
         lax.psum(shard_up.astype(jnp.bfloat16), "ctx").astype(jnp.float32),
         lax.psum(shard_down.astype(jnp.bfloat16), "ctx").astype(jnp.float32),

time: 1690 us -> 1820 us (1.077)
  waiting for transfers between devices: 705 us -> 815 us
    all_gather x0 -> x1, waiting for transfers between devices: none -> 97.7 us  [body(): lax.all_gather(shard_qkv.astype(jnp.bfloat16), 'ctx')]
    unnamed x97 -> x99, local copies, waits for them, and re-layouts: 81 us -> 80.3 us
  transfers between devices with their start and end apart: 13 -> 14, of which waited for: 10 -> 11; matrix products, arithmetic and copies ran while one was open for 26% -> 25% of each run, Pallas kernels for 0% -> 0%
where the time goes in v1:
time: 1820 us; the launch traced here: 1810 us
  waiting for transfers between devices  815 us (45%)
  matrix products  581 us (32%)
  local copies, waits for them, and re-layouts  207 us (11%)
  other arithmetic  144 us (8%)
  blocking collectives  48.4 us (3%)
    dot_general x16, matrix products, head_scores(): jnp.einsum('qhd,khd->hqk', query_heads, key_heads, preferred_element_type...  152 us
    reduce_scatter x1, waiting for transfers between devices, body(): lax.psum_scatter(dkeys_all.astype(jnp.bfloat16), 'ctx', scatter_dimension...  110 us
    reduce_scatter x1, waiting for transfers between devices, body(): lax.psum_scatter(grad_qkv.astype(jnp.bfloat16), 'fsdp', scatter_dimension...  101 us
    all_gather x1, waiting for transfers between devices, body(): lax.all_gather(w_qkv.astype(bf16), 'fsdp', axis=0, tiled=True)  100 us
    all_gather x1, waiting for transfers between devices, body(): lax.all_gather(shard_qkv.astype(jnp.bfloat16), 'ctx')  97.7 us
    dot_general x8, matrix products, back_step(): jnp.einsum('qhd,khd->hqk', dattn_heads, key_set[1], preferred_element_typ...  88.4 us
    all_gather x1, waiting for transfers between devices, body(): lax.all_gather(keys_here, 'ctx', axis=0, tiled=True)  83.4 us
    reduce_scatter x1, waiting for transfers between devices, body(): lax.psum_scatter(dvalues_all.astype(jnp.bfloat16), 'ctx', scatter_dimensi...  81 us
  transfers between devices with their start and end apart: 14, of which 11 were waited for; matrix products, arithmetic and copies ran while one was open for 25% of the time, Pallas kernels for 0%

profile of v1, /device:TPU:0, one launch (start us, length us, event | category | flops | bytes accessed | tf_op | source)
XLA Modules:
  0.0 1813.1 jit_solution(2025862214605842196)
XLA Ops:
  13.6 100.2 %all-gather.9.cloned.1.call-done = bf16[1280,3840]{1,0:T(8,128)(2,1)} async-done(((bf16[320,3840]{1,0:T(8,128)(2,1)}), bf16[1280,3840]{1,0:T(8,128)(2,1)}) %all-gather.9.cloned.1.call-update) | async-done | bytes 9830416 | tf_op jit(solution)/shard_map/all_gather | solution.py:87
  113.8 11.3 fusion.97
  143.0 83.4 %all-gather.13.cloned.1.call-done = bf16[4096,1280]{1,0:T(8,128)(2,1)} async-done(((bf16[512,1280]{1,0:T(8,128)(2,1)}), bf16[4096,1280]{1,0:T(8,128)(2,1)}) %all-gather.13.cloned.1.call-update) | async-done | bytes 10485776 | tf_op jit(solution)/shard_map/all_gather | solution.py:110
  226.4 14.5 copy.59
  240.9 15.1 copy.93
  256.0 16.3 copy.63
  272.3 11.7 copy.61
  284.0 42.4 %all-gather.11.cloned.1.call-done = bf16[4096,1280]{1,0:T(8,128)(2,1)} async-done(((bf16[512,1280]{1,0:T(8,128)(2,1)}), bf16[4096,1280]{1,0:T(8,128)(2,1)}) %all-gather.11.cloned.1.call-update) | async-done | bytes 10485776 | tf_op jit(solution)/shard_map/all_gather | solution.py:111
  326.4 29.8 %reshape.411 = bf16[8,512,16,80]{3,2,1,0:T(8,128)(2,1)} reshape(bf16[4096,1280]{1,0:T(8,128)(2,1)} %all-gather.11.cloned.1.call-done) | data formatting | bytes 20971520 | tf_op jit(solution)/shard_map/reshape | solution.py:118
  356.2 21.7 %copy.62 = bf16[8,512,16,80]{1,3,2,0:T(8,128)(2,1)} copy(bf16[8,512,16,80]{3,2,1,0:T(8,128)(2,1)} %reshape.411) | data formatting | bytes 20971520
  378.0 150.3 %while.39 = (s32[]{:T(128)}, f32[16,512]{1,0:T(8,128)S(1)}, f32[16,512]{1,0:T(8,128)S(1)}, s32[8,512]{1,0:T(8,128)S(1)}, s32[512]{0:T(512)S(1)}, /*index=5*/s32[...) while((s32[]{:T(128)}, f32[16,512]{1,0:T(8,128)S(1)}, ...), condition=%wide.region_4.5_spmd.clone, body=%wide.region_1.4_spmd.clone.sunk | while | flops 693150208 | bytes 37405832 | solution.py:135
  378.4 9.6 fusion.140
  397.1 9.5 fusion.140
  415.7 9.5 fusion.140
  425.2 9.4 fusion.141
  435.1 9.5 fusion.140
  444.7 9.2 fusion.141
  454.3 9.5 fusion.140
  472.9 9.5 fusion.140
  491.5 9.5 fusion.140
  510.1 9.5 fusion.140
  528.4 95.0 %while.40 = (s32[]{:T(128)}, f32[512,16,80]{0,2,1:T(8,128)}, bf16[8,512,16,80]{1,3,2,0:T(8,128)(2,1)}, s32[8,512]{1,0:T(8,128)S(1)}, s32[512]{0:T(512)S(1)}, /*i...) while((s32[]{:T(128)}, f32[512,16,80]{0,2,1:T(8,128)}, ...), condition=%wide.region_6.7_spmd.clone, body=%wide.region_5.6_spmd.clone.sunk | while | flops 1357120000 | bytes 13157527 | solution.py:148
  543.1 8.8 bitcast_add_fusion.4
  555.0 8.8 bitcast_add_fusion.4
  578.8 8.8 bitcast_add_fusion.4
  590.7 8.8 bitcast_add_fusion.4
  655.4 418.2 %while.41 = (s32[]{:T(128)}, f32[512,16,80]{0,2,1:T(8,128)}, bf16[8,512,1280]{2,1,0:T(8,128)(2,1)}, bf16[8,512,1280]{2,1,0:T(8,128)(2,1)}, bf16[8,512,16,80]{1,3...) while((s32[]{:T(128)}, f32[512,16,80]{0,2,1:T(8,128)}, ...), condition=%wide.region_11.12_spmd.clone, body=%wide.region_10.11_spmd.clone.sunk | while | flops 3391357440 | bytes 103924920 | solution.py:191
  655.4 9.5 fusion.156
  665.2 11.1 fusion.157
  683.0 9.9 fusion.158
  707.1 9.4 fusion.156
  716.9 11.1 fusion.157
  735.4 9.9 fusion.158
  759.4 9.5 fusion.156
  769.2 11.1 fusion.157
  787.7 9.9 fusion.158
  811.8 9.5 fusion.156
  821.6 11.0 fusion.157
  840.1 9.9 fusion.158
  864.1 9.5 fusion.156
  874.0 11.0 fusion.157
  892.5 9.9 fusion.158
  916.5 9.5 fusion.156
  926.3 11.0 fusion.157
  944.8 9.9 fusion.158
  968.8 9.5 fusion.156
  978.6 11.0 fusion.157
  997.2 9.9 fusion.158
  1021.2 9.5 fusion.156
  1031.0 11.0 fusion.157
  1049.5 9.9 fusion.158
  1100.7 81.0 %reduce-scatter.9.cloned.1.call-done = bf16[512,1280]{1,0:T(8,128)(2,1)} async-done(((bf16[4096,1280]{1,0:T(8,128)(2,1)}), bf16[512,1280]{1,0:T(8,128)(2,1)}) %reduce-scatter.9.cloned.1.call-update) | async-done | bytes 1310736 | tf_op jit(solution)/shard_map/reduce_scatter | solution.py:198
  1181.7 110.1 %reduce-scatter.7.cloned.1.call-done = bf16[512,1280]{1,0:T(8,128)(2,1)} async-done(((bf16[4096,1280]{1,0:T(8,128)(2,1)}), bf16[512,1280]{1,0:T(8,128)(2,1)}) %reduce-scatter.7.cloned.1.call-update) | async-done | bytes 1310736 | tf_op jit(solution)/shard_map/reduce_scatter | solution.py:195
  1291.9 9.7 convolution_convert_fusion
  1301.7 37.3 %reduce-scatter.13.cloned.1.call-done = bf16[320,1280]{1,0:T(8,128)(2,1)} async-done(((bf16[1280,1280]{1,0:T(8,128)(2,1)}), bf16[320,1280]{1,0:T(8,128)(2,1)}) %reduce-scatter.13.cloned.1.call-update) | async-done | bytes 819216 | tf_op jit(solution)/shard_map/reduce_scatter | solution.py:227
  1338.9 48.5 %reduce-scatter.15.cloned.1.call-done = bf16[320,1280]{1,0:T(8,128)(2,1)} async-done(((bf16[1280,1280]{1,0:T(8,128)(2,1)}), bf16[320,1280]{1,0:T(8,128)(2,1)}) %reduce-scatter.15.cloned.1.call-update) | async-done | bytes 819216 | tf_op jit(solution)/shard_map/reduce_scatter | solution.py:230
  1387.4 48.7 %reduce-scatter.17.cloned.1.call-done = bf16[320,1280]{1,0:T(8,128)(2,1)} async-done(((bf16[1280,1280]{1,0:T(8,128)(2,1)}), bf16[320,1280]{1,0:T(8,128)(2,1)}) %reduce-scatter.17.cloned.1.call-update) | async-done | bytes 819216 | tf_op jit(solution)/shard_map/reduce_scatter | solution.py:233
  1436.4 100.9 %reduce-scatter.11.cloned.1.call-done = bf16[320,3840]{1,0:T(8,128)(2,1)} async-done(((bf16[1280,3840]{1,0:T(8,128)(2,1)}), bf16[320,3840]{1,0:T(8,128)(2,1)}) %reduce-scatter.11.cloned.1.call-update) | async-done | bytes 2457616 | tf_op jit(solution)/shard_map/reduce_scatter | solution.py:224
  1544.2 63.3 %all-reduce.3.cloned.1.call-done = (bf16[320,1280]{1,0:T(8,128)(2,1)}, bf16[320,1280]{1,0:T(8,128)(2,1)}, bf16[320,1280]{1,0:T(8,128)(2,1)}) async-done(((bf16[320,1280]{1,0:T(8,128)(2,1)}, bf16[320,1280]{1,0:T(8,128)(2,1)}, bf16[320,1280]{1,0:T(8,128)(2,1)}), (bf16[320,1280]{1,0:T(8,128)(2,1)}, bf16[320,1280]{1,0:T(8,128)(2,1)}, bf16[320,1280]{1,0:T(8,128)(2,1)})) %all-reduce.3.cloned.1.call-update) | async-done | bytes 2457616 | tf_op jit(solution)/shard_map/psum | solution.py:239
  1622.8 10.8 fusion.56
  1633.6 48.4 %psum.31 = f32[2640]{0:T(1024)S(1)} all-reduce(f32[2640]{0:T(1024)S(1)} %pad_maximum_fusion.3), channel_id=1, replica_groups=mesh['ctx'=8,'fsdp'=4] {'ctx','fsdp'}, use_global_device_ids=true, to_apply=%region_26.27 | all-reduce | flops 2640 | bytes 21120 | tf_op jit(solution)/shard_map/psum | solution.py:218
  1687.0 97.7 %all-gather.21.cloned.1.call-done = bf16[2560,3840]{1,0:T(8,128)(2,1)} async-done(((bf16[320,3840]{1,0:T(8,128)(2,1)}), bf16[2560,3840]{1,0:T(8,128)(2,1)}) %all-gather.21.cloned.1.call-update) | async-done | bytes 19660816 | tf_op jit(solution)/shard_map/all_gather | solution.py:238
  1784.7 10.9 reduce_sum.98
  1795.6 10.7 fusion.93
  (339 shorter events, 399.4 us)
Async XLA Ops:
  7.2 106.6 %all-gather.9.cloned.1.call-start = ((), (), s32[]{:S(2)}) async-start(), calls=%async_computation.6 | async-start | bytes 12288000 | tf_op jit(solution)/shard_map/all_gather | solution.py:87
  11.3 1.3 copy-start.1
  11.3 1.7 copy-start.25
  11.3 215.1 %all-gather.13.cloned.1.call-start = ((), (), s32[]{:S(2)}) async-start(), calls=%async_computation.8 | async-start | bytes 11796480 | tf_op jit(solution)/shard_map/all_gather | solution.py:110
  13.0 112.2 %copy-start.36 = (f32[512]{0:T(512)}, f32[512]{0:T(512)S(1)}, u32[]{:S(2)}) copy-start(f32[512]{0:T(512)S(1)} %add_rsqrt_fusion.1) | copy-start | bytes 6148
  13.6 111.6 %copy-start.29 = (f32[1280]{0:T(1024)}, f32[1280]{0:T(1024)S(1)}, u32[]{:S(2)}) copy-start(f32[1280]{0:T(1024)S(1)} %get-tuple-element.484) | copy-start | bytes 15364
  126.8 1.4 copy-start.9
  126.8 2.5 copy-start.11
  126.9 199.6 %all-gather.11.cloned.1.call-start = ((), (), s32[]{:S(2)}) async-start(), calls=%async_computation.7 | async-start | bytes 11796480 | tf_op jit(solution)/shard_map/all_gather | solution.py:111
  127.6 498.8 %all-gather.15.cloned.1.call-start = ((), (), s32[]{:S(2)}) async-start(), calls=%async_computation.9 | async-start | bytes 4096000 | tf_op jit(solution)/shard_map/all_gather | solution.py:88
  129.2 1.7 copy-start.13
  129.2 503.1 %all-gather.17.cloned.1.call-start = ((), (), s32[]{:S(2)}) async-start(), calls=%async_computation.10 | async-start | bytes 4096000 | tf_op jit(solution)/shard_map/all_gather | solution.py:89
  130.3 2.3 copy-start.43
  130.3 508.3 %all-gather.19.cloned.1.call-start = ((), (), s32[]{:S(2)}) async-start(), calls=%async_computation.11 | async-start | bytes 4096000 | tf_op jit(solution)/shard_map/all_gather | solution.py:90
  131.9 1049.8 %reduce-scatter.9.cloned.1.call-start = ((), (), s32[]{:S(2)}) async-start(), calls=%async_computation.13 | async-start | bytes 11796480 | tf_op jit(solution)/shard_map/reduce_scatter | solution.py:198
  132.6 5.3 copy-start.38
  623.3 3.1 copy-start.2
  626.4 5.9 copy-start.27
  632.3 14.0 copy-start.33
  632.4 6.2 copy-start.19
  638.6 5.1 copy-start.5
  638.6 5.1 copy-start.40
  643.7 2.6 copy-start.44
  646.4 2.7 copy-start.4
  647.0 1.6 copy-start.7
  1073.6 218.2 %reduce-scatter.7.cloned.1.call-start = ((), (), s32[]{:S(2)}) async-start(), calls=%async_computation.12 | async-start | bytes 11796480 | tf_op jit(solution)/shard_map/reduce_scatter | solution.py:195
  1073.7 1.7 copy-start.8
  1074.4 264.5 %reduce-scatter.13.cloned.1.call-start = ((), (), s32[]{:S(2)}) async-start(), calls=%async_computation.15 | async-start | bytes 4096000 | tf_op jit(solution)/shard_map/reduce_scatter | solution.py:227
  1080.3 1.7 copy-start.6
  1080.3 1.7 copy-start.28
  1080.3 1.7 copy-start.34
  1080.3 307.1 %reduce-scatter.15.cloned.1.call-start = ((), (), s32[]{:S(2)}) async-start(), calls=%async_computation.16 | async-start | bytes 4096000 | tf_op jit(solution)/shard_map/reduce_scatter | solution.py:230
  1087.1 1.3 copy-start.20
  1087.1 349.0 %reduce-scatter.17.cloned.1.call-start = ((), (), s32[]{:S(2)}) async-start(), calls=%async_computation.17 | async-start | bytes 4096000 | tf_op jit(solution)/shard_map/reduce_scatter | solution.py:233
  1093.8 1.8 copy-start
  1093.8 1.8 copy-start.39
  1093.8 443.5 %reduce-scatter.11.cloned.1.call-start = ((), (), s32[]{:S(2)}) async-start(), calls=%async_computation.14 | async-start | bytes 12288000 | tf_op jit(solution)/shard_map/reduce_scatter | solution.py:224
  1099.0 192.9 %copy-start.3 = (bf16[1,512,1280]{2,1,0:T(8,128)(2,1)S(1)}, bf16[1,512,1280]{2,1,0:T(8,128)(2,1)}, u32[]{:S(2)}) copy-start(bf16[1,512,1280]{2,1,0:T(8,128)(2,1)} %param.24) | copy-start | bytes 3932164
  1099.0 192.9 %copy-start.30 = (f32[1280]{0:T(1024)S(1)}, f32[1280]{0:T(1024)}, u32[]{:S(2)}) copy-start(f32[1280]{0:T(1024)} %copy-done.29) | copy-start | bytes 15364
  1099.0 192.9 %copy-start.37 = (f32[512]{0:T(512)S(1)}, f32[512]{0:T(512)}, u32[]{:S(2)}) copy-start(f32[512]{0:T(512)} %copy-done.36) | copy-start | bytes 6148
  1100.7 200.9 %copy-start.21 = (bf16[512,1280]{1,0:T(8,128)(2,1)}, bf16[512,1280]{1,0:T(8,128)(2,1)S(1)}, u32[]{:S(2)}) copy-start(bf16[512,1280]{1,0:T(8,128)(2,1)S(1)} %copy.70) | copy-start | bytes 3932164
  1301.6 235.7 %copy-start.26 = (f32[2640]{0:T(1024)S(1)}, f32[2640]{0:T(1024)}, u32[]{:S(2)}) copy-start(f32[2640]{0:T(1024)} %param.39) | copy-start | bytes 31684
  1301.6 306.0 %all-reduce.3.cloned.1.call-start = ((), (), s32[]{:S(2)}) async-start(), calls=%async_computation.19 | async-start | bytes 4915200 | tf_op jit(solution)/shard_map/psum | solution.py:239
  1436.2 348.5 %all-gather.21.cloned.1.call-start = ((), (), s32[]{:S(2)}) async-start(), calls=%async_computation.18 | async-start | bytes 22118400 | tf_op jit(solution)/shard_map/all_gather | solution.py:238
  1537.4 70.2 %copy-start.10 = (f32[320,1280]{1,0:T(8,128)S(1)}, f32[320,1280]{1,0:T(8,128)}, u32[]{:S(2)}) copy-start(f32[320,1280]{1,0:T(8,128)} %param.30) | copy-start | bytes 4915204
  1607.6 5.6 copy-start.12
  1607.6 5.6 copy-start.15
  1607.6 5.6 copy-start.16
  1607.6 5.6 copy-start.24
  1613.2 3.5 copy-start.14
  1613.2 3.5 copy-start.17
  1613.2 4.7 copy-start.18
  1613.2 5.0 copy-start.23
  1618.3 3.5 copy-start.22
  1618.3 3.5 copy-start.41
  1618.3 4.5 copy-start.42
  1622.8 10.9 copy-start.35
  1622.8 59.2 %copy-start.31 = (f32[2640]{0:T(1024)S(1)}, f32[2640]{0:T(1024)}, u32[]{:S(2)}) copy-start(f32[2640]{0:T(1024)} %param.40) | copy-start | bytes 31684
  1622.8 59.2 %copy-start.32 = (f32[2640]{0:T(1024)S(1)}, f32[2640]{0:T(1024)}, u32[]{:S(2)}) copy-start(f32[2640]{0:T(1024)} %param.41) | copy-start | bytes 31684
Sparse Core Ops, SparseCore 0:
  11.5 102.2 all-gather.8
  127.0 99.4 all-gather.12
  228.7 97.7 all-gather.10
  328.7 43.4 all-gather.14
  374.4 45.0 all-gather.16
  421.8 45.0 all-gather.18
  1073.7 107.9 reduce-scatter.8
  1184.0 107.7 reduce-scatter.6
  1295.5 43.4 reduce-scatter.12
  1342.4 45.0 reduce-scatter.14
  1391.0 45.0 reduce-scatter.16
  1439.1 98.1 reduce-scatter.10
  1539.9 67.6 all-reduce.2
  1609.2 175.4 all-gather.20
